TPU v7x, 32 devices: a whole 2x2x4 slice. The times are simulated.
32 devices in a mesh: split: 8 (over z, y), group: 4 (over x, core).
Axes of the slice: x: 2, y: 2, z: 4, core: 2. Of those that a mesh axis runs over, the one named last changes fastest.
Arguments:
- field: float32 [128, 512, 512], P(('group', 'split')), parts along dimension 0, may hold values from -8 to 8
- selector: int32 [128], P('group'), parts along dimension 0, may hold values from 0 to 3
- profiles: float32 [16, 512], P('group'), parts along dimension 0, may hold values from 0.5 to 1.5
- row_gain: float32 [2048], P('group'), parts along dimension 0, may hold values from 0.5 to 1.5
- levels: int32 [16], P('group'), parts along dimension 0, may hold values from 5 to 7
Outputs:
- surplus: float32 [128, 512, 512], P(('group', 'split')), parts along dimension 0
There are 4 independent parts, one for each index of `group`. A program takes and returns all parts, laid end to end along the dimension named above; each array names one. Nothing has to cross between parts.
All inputs are finite; a program needn't handle non-finite values.
Results may differ from a plain program's by a relative error of at most 0.00012.
Values sent between devices are 32-bit elements; how exact they have to be, the bound alone decides.
A program may use at most 192 MiB of HBM per device.

v0:
```python
import functools

import jax
import jax.numpy as jnp
import numpy as np
from jax import lax
from jax.experimental import pallas as pl
from jax.experimental.pallas import tpu as pltpu
from jax.sharding import PartitionSpec as P

N3 = 32
N4 = 16
CHUNKS = 8
STEP = 16
PAD = 8
HALF = 0.5


def low_bit(x):
    return x & -x


def lift_matrix(count):
    table = np.eye(count, dtype=np.float64)
    for j in range(1, count):
        s = low_bit(j)
        table[j, j - s] -= 0.5
        table[j, (j + s) % count] -= 0.5
    return table


def three_parts(x):
    high = x.astype(jnp.bfloat16)
    rest = x - high.astype(jnp.float32)
    middle = rest.astype(jnp.bfloat16)
    low = (rest - middle.astype(jnp.float32)).astype(jnp.bfloat16)
    return high, middle, low


def kernel(
    n,
    field,
    selector,
    profiles,
    row_gain,
    levels,
    second_table,
    merged_table,
    out,
    u,
    diffused,
    parts,
    lifted,
    result,
    f_prev,
    f_next,
    y_next,
    y_left,
    y_right,
    coefs,
    gains,
    local_sem,
    send_sem,
    recv_sem,
    out_sem,
):
    planes, rows, width = field.shape
    chunk = rows // CHUNKS
    me = lax.axis_index("split")
    total = n * planes
    rank = (me + n // 2) % n
    odd = me % 2 == 1
    even = me % 2 == 0
    ahead = (me + 1) % n
    behind = (me + n - 1) % n

    barrier = pltpu.get_barrier_semaphore()

    def greet(k, carry):
        pl.semaphore_signal(
            barrier,
            inc=1,
            device_id={"split": (me + k) % n},
            device_id_type=pl.DeviceIdType.MESH,
        )
        return carry

    lax.fori_loop(1, n, greet, 0)

    loads = [
        pltpu.make_async_copy(field, u.at[:, pl.ds(PAD, rows), :], local_sem.at[0]),
        pltpu.make_async_copy(
            field.at[:, pl.ds(rows - PAD, PAD), :], u.at[:, pl.ds(0, PAD), :], local_sem.at[1]
        ),
        pltpu.make_async_copy(
            field.at[:, pl.ds(0, PAD), :], u.at[:, pl.ds(rows + PAD, PAD), :], local_sem.at[2]
        ),
    ]
    for load in loads:
        load.start()

    def at(c):
        return pl.ds(pl.multiple_of(c * chunk, chunk), chunk)

    def remote(source, target, c, send, slot, device):
        return pltpu.make_async_remote_copy(
            src_ref=source,
            dst_ref=target.at[at(c), :],
            send_sem=send_sem.at[send, c],
            recv_sem=recv_sem.at[slot, c],
            device_id={"split": device},
            device_id_type=pl.DeviceIdType.MESH,
        )

    def last_plane(c):
        return remote(field.at[planes - 1, at(c), :], f_prev, c, 0, 0, ahead)

    def first_plane(c):
        return remote(field.at[0, at(c), :], f_next, c, 1, 1, behind)

    def own(c, target, send, slot, device):
        return remote(lifted.at[0, at(c), :], target, c, send, slot, device)

    def to_pair(c):
        return own(c, y_left, 2, 3, ahead)

    def to_behind(c):
        return own(c, y_next, 2, 2, behind)

    def relay(c):
        return remote(y_left.at[at(c), :], y_next, c, 3, 2, (me + n - 2) % n)

    sends = [(even, to_pair), (odd, to_behind)]
    s, slot = 2, 4
    while s < n:
        sends.append(
            (
                rank % (2 * s) == 0,
                functools.partial(
                    own, target=y_left, send=slot, slot=3, device=(me + s) % n
                ),
            )
        )
        if 2 * s < n:
            sends.append(
                (
                    rank % (2 * s) == 0,
                    functools.partial(
                        own, target=y_right, send=slot + 1, slot=4, device=(me + n - s) % n
                    ),
                )
            )
        s, slot = 2 * s, slot + 2

    pl.semaphore_wait(barrier, n - 1)

    def each(step):
        def body(c, carry):
            step(c)
            return carry

        lax.fori_loop(0, CHUNKS, body, 0)

    each(lambda c: last_plane(c).start())
    each(lambda c: first_plane(c).start())

    def power(d):
        return jnp.exp2(jnp.full((1, width), levels[d].astype(jnp.float32), jnp.float32))

    powers = [power(d) for d in range(4)]
    scale = 0.2 / (powers[0] + powers[1] + powers[2] + powers[3])
    w = [HALF * scale * power_d for power_d in powers]
    fields = profiles.shape[0]

    def profile(q):
        chosen = selector[(me * planes + q + total) % total]
        row = jnp.zeros((1, width), jnp.float32)
        for k in range(fields):
            row = row + jnp.where(chosen == k, profiles[pl.ds(k, 1), :], 0.0)
        return row

    lane = lax.broadcasted_iota(jnp.int32, (1, width), 1) % N4
    first_lane = lane == 0
    final_lane = lane == N4 - 1

    def shifted(x, by):
        return pltpu.roll(x, by % width, 1)

    def after(x):
        return jnp.where(final_lane, shifted(x, N4 - 1), shifted(x, -1))

    def before(x):
        return jnp.where(first_lane, shifted(x, 1 - N4), shifted(x, 1))

    chosen_rows = [profile(q) for q in range(-1, planes + 1)]
    for q in range(planes):
        low, mid, high = chosen_rows[q : q + 3]
        wide = jnp.broadcast_to(mid, (8, width))

        def pair(x):
            return (wide + x)[0:1]

        kinds = [
            w[0] * (mid + low),
            w[0] * (mid + high),
            w[2] * pair(shifted(wide, -N4)),
            w[2] * pair(shifted(wide, N4)),
            w[3] * pair(after(wide)),
            w[3] * pair(before(wide)),
            w[1] * mid,
        ]
        for k, row in enumerate(kinds):
            coefs[q, pl.ds(k, 1), :] = row
    gain = jnp.broadcast_to(row_gain[...], (128, rows))
    gains[0] = jnp.transpose(gain)
    gains[1] = jnp.transpose(gain + pltpu.roll(gain, rows - 1, 1))
    gains[2] = jnp.transpose(gain + pltpu.roll(gain, 1, 1))

    for load in loads:
        load.wait()

    def column(k, where):
        return jnp.concatenate([gains[k, where, :]] * (width // 128), axis=1)

    def diffuse(q, i):
        start = pl.multiple_of(i * STEP, STEP)
        here = pl.ds(start, STEP)
        inner = pl.ds(pl.multiple_of(start + PAD, 8), STEP)
        block = u[q, pl.ds(start, STEP + 2 * PAD), :]
        center = block[PAD : PAD + STEP]
        up = block[PAD - 1 : PAD - 1 + STEP]
        down = block[PAD + 1 : PAD + 1 + STEP]
        lower = u[jnp.maximum(q - 1, 0), inner, :]
        upper = u[jnp.minimum(q + 1, planes - 1), inner, :]

        def k(index):
            return coefs[q, pl.ds(index, 1), :]

        flow = k(0) * (lower - center) + k(1) * (upper - center)
        flow = flow + k(2) * (shifted(center, -N4) - center)
        flow = flow + k(3) * (shifted(center, N4) - center)
        flow = flow + k(4) * (after(center) - center) + k(5) * (before(center) - center)
        along = column(1, here) * (down - center) + column(2, here) * (up - center)
        diffused[q, here, :] = center + column(0, here) * flow + k(6) * along

    def join(q, c, index, other):
        def body(i, carry):
            start = pl.multiple_of(c * chunk + i * STEP, STEP)
            here = pl.ds(start, STEP)
            center = u[q, pl.ds(pl.multiple_of(start + PAD, 8), STEP), :]
            change = coefs[q, pl.ds(index, 1), :] * (other[here, :] - center)
            diffused[q, here, :] = diffused[q, here, :] + column(0, here) * change
            return carry

        lax.fori_loop(0, chunk // STEP, body, 0, unroll=True)

    def lift_lanes(q, c):
        where = at(c)
        total_ = jnp.zeros((chunk, width), jnp.float32)
        for part in reversed(three_parts(diffused[q, where, :])):
            total_ = total_ + jnp.dot(
                part, merged_table[...], preferred_element_type=jnp.float32
            )
        for k, part in enumerate(three_parts(total_)):
            parts[k, where, :] = part

    def lift_rows(q):
        block = min(128, rows)

        def body(i, carry):
            where = pl.ds(pl.multiple_of(i * block, block), block)
            table = second_table[where, :]
            total_ = jnp.dot(table, parts[2], preferred_element_type=jnp.float32)
            total_ = total_ + jnp.dot(table, parts[1], preferred_element_type=jnp.float32)
            total_ = total_ + jnp.dot(table, parts[0], preferred_element_type=jnp.float32)
            lifted[q, where, :] = total_
            return carry

        lax.fori_loop(0, rows // block, body, 0)

    def base(j, carry):
        diffuse(j // (rows // STEP), j % (rows // STEP))
        return carry

    lax.fori_loop(0, planes * (rows // STEP), base, 0, unroll=2)

    def inner_plane(q, carry):
        each(lambda c: lift_lanes(q, c))
        lift_rows(q)
        return carry

    lax.fori_loop(1, planes - 1, inner_plane, 0)

    def first_arrived(c):
        last_plane(c).wait_recv()
        join(0, c, 0, f_prev)
        lift_lanes(0, c)

    each(first_arrived)
    lift_rows(0)

    for holds, copy in sends:

        @pl.when(holds)
        def _(copy=copy):
            each(lambda c: copy(c).start())

    def last_arrived(c):
        first_plane(c).wait_recv()
        join(planes - 1, c, 1, f_next)
        lift_lanes(planes - 1, c)

    each(last_arrived)
    lift_rows(planes - 1)

    def store(q, c):
        return pltpu.make_async_copy(
            result.at[q, at(c), :], out.at[q, at(c), :], out_sem.at[q, c]
        )

    for q in range(1, planes):
        s = low_bit(q)
        if q + s < planes:

            def whole(c, q=q, s=s):
                where = at(c)
                result[q, where, :] = lifted[q, where, :] - HALF * (
                    lifted[q - s, where, :] + lifted[q + s, where, :]
                )
                store(q, c).start()

            each(whole)

    def finish(c):
        where = at(c)
        to_behind(c).wait_recv()
        for q in range(1, planes):
            s = low_bit(q)
            if q + s == planes:
                result[q, where, :] = lifted[q, where, :] - HALF * (
                    lifted[q - s, where, :] + y_next[where, :]
                )
                store(q, c).start()

        @pl.when(odd)
        def _():
            result[0, where, :] = lifted[0, where, :] - HALF * (
                y_left[where, :] + y_next[where, :]
            )

        @pl.when(rank == n // 2)
        def _():
            to_pair(c).wait_recv()
            result[0, where, :] = lifted[0, where, :] - y_left[where, :]

        @pl.when(rank == 0)
        def _():
            result[0, where, :] = lifted[0, where, :]

        @pl.when(even & (rank % (n // 2) != 0))
        def _():
            to_pair(c).wait_recv()
            own(c, y_right, 2, 4, ahead).wait_recv()
            result[0, where, :] = lifted[0, where, :] - HALF * (
                y_left[where, :] + y_right[where, :]
            )

        store(0, c).start()

    def pass_on(c):
        @pl.when(odd)
        def _():
            to_pair(c).wait_recv()
            relay(c).start()

    pass_on(0)

    def turn(c, carry):
        pass_on(c)
        finish(c - 1)
        return carry

    lax.fori_loop(1, CHUNKS, turn, 0)
    finish(CHUNKS - 1)

    each(lambda c: last_plane(c).wait_send())
    each(lambda c: first_plane(c).wait_send())
    for holds, copy in [*sends, (odd, relay)]:

        @pl.when(holds)
        def _(copy=copy):
            each(lambda c: copy(c).wait_send())

    for q in range(planes):
        each(lambda c, q=q: store(q, c).wait())


def on_device(field, selector, profiles, row_gain, levels):
    planes, rows, width = field.shape
    n = lax.axis_size("split")
    second_table = jnp.asarray(lift_matrix(rows).astype(jnp.bfloat16))
    merged_table = jnp.asarray(np.kron(lift_matrix(N3), lift_matrix(N4)).T.astype(jnp.bfloat16))
    kinds = 4 + 2 * n.bit_length()
    plane = pltpu.VMEM((rows, width), jnp.float32)
    block = pltpu.VMEM((planes, rows, width), jnp.float32)
    return pl.pallas_call(
        functools.partial(kernel, n),
        out_shape=jax.ShapeDtypeStruct(field.shape, jnp.float32),
        in_specs=[
            pl.BlockSpec(memory_space=pl.ANY),
            pl.BlockSpec(memory_space=pltpu.SMEM),
            pl.BlockSpec(memory_space=pltpu.VMEM),
            pl.BlockSpec(memory_space=pltpu.VMEM),
            pl.BlockSpec(memory_space=pltpu.SMEM),
            pl.BlockSpec(memory_space=pltpu.VMEM),
            pl.BlockSpec(memory_space=pltpu.VMEM),
        ],
        out_specs=pl.BlockSpec(memory_space=pl.ANY),
        scratch_shapes=[
            pltpu.VMEM((planes, rows + 2 * PAD, width), jnp.float32),
            block,
            pltpu.VMEM((3, rows, width), jnp.bfloat16),
            block,
            block,
            plane,
            plane,
            plane,
            plane,
            plane,
            pltpu.VMEM((planes, 8, width), jnp.float32),
            pltpu.VMEM((3, rows, 128), jnp.float32),
            pltpu.SemaphoreType.DMA((3,)),
            pltpu.SemaphoreType.DMA((kinds, CHUNKS)),
            pltpu.SemaphoreType.DMA((5, CHUNKS)),
            pltpu.SemaphoreType.DMA((planes, CHUNKS)),
        ],
        compiler_params=pltpu.CompilerParams(
            collective_id=0, has_side_effects=True, vmem_limit_bytes=50 * 1024 * 1024
        ),
        name="step_and_lift",
    )(
        field,
        selector,
        profiles,
        row_gain.reshape(1, rows),
        levels,
        second_table,
        merged_table,
    )


def solution(mesh):
    placed = (
        P(("group", "split"), None, None),
        P("group"),
        P("group", None),
        P("group"),
        P("group"),
    )
    return jax.shard_map(
        on_device,
        mesh=mesh,
        in_specs=placed,
        out_specs=P(("group", "split"), None, None),
        check_vma=False,
    )
```

profile of v0, /device:TPU:4, one launch (start us, length us, event | category | flops | bytes accessed | tf_op | source)
XLA Modules:
  0.0 94.0 jit_solution(231177766030387056)
XLA Ops:
  0.0 0.0 copy-start
  0.0 1.0 %copy-done = bf16[512,512]{1,0:T(8,128)(2,1)S(1)} copy-done((bf16[512,512]{1,0:T(8,128)(2,1)S(1)}, bf16[512,512]{1,0:T(8,128)(2,1)}, u32[]{:S(2)}) %copy-start) | copy-done | bytes 524312
  1.0 0.0 copy-start.1
  1.0 1.0 %copy-done.1 = bf16[512,512]{1,0:T(8,128)(2,1)S(1)} copy-done((bf16[512,512]{1,0:T(8,128)(2,1)S(1)}, bf16[512,512]{1,0:T(8,128)(2,1)}, u32[]{:S(2)}) %copy-start.1) | copy-done | bytes 524312
  2.1 0.0 copy-start.2
  2.1 0.7 copy-done.2
  2.8 0.0 copy-start.3
  2.8 0.7 copy-done.3
  3.5 0.0 copy-start.4
  3.5 0.7 copy-done.4
  4.1 0.0 copy-start.5
  4.1 0.7 copy-done.5
  4.8 84.6 %step_and_lift.1 = f32[4,512,512]{2,1,0:T(8,128)} custom-call(f32[4,512,512]{2,1,0:T(8,128)} %field.1, s32[32]{0:T(128)S(1)} %copy-done.4, f32[4,512]{1,0:T(4,128)S(1)} %copy-done.2, f32[1,512]{1,0:T(1,128)S(1)} %bitcast.1, s32[4]{0:T(128)S(1)} %copy-done.5, bf16[512,512]{1,0:T(8,128)(2,1)S(1)} %copy-done.1, bf16[512,512]{1,0:T(8,128)(2,1)S(1)} %copy-done), custom_call_target="tpu_custom_call" | custom-call | tf_op jit(solution)/shard_map/step_and_lift/pallas_call | solution.py:406
  89.4 4.6 %copy.9 = f32[4,512,512]{2,1,0:T(8,128)} copy(f32[4,512,512]{2,1,0:T(8,128)} %step_and_lift.1) | data formatting | bytes 8388608
Async XLA Ops:
  0.0 1.0 %copy-start = (bf16[512,512]{1,0:T(8,128)(2,1)S(1)}, bf16[512,512]{1,0:T(8,128)(2,1)}, u32[]{:S(2)}) copy-start(bf16[512,512]{1,0:T(8,128)(2,1)} %constant.5.clone.merged_table) | copy-start | bytes 1572868
  1.0 1.0 %copy-start.1 = (bf16[512,512]{1,0:T(8,128)(2,1)S(1)}, bf16[512,512]{1,0:T(8,128)(2,1)}, u32[]{:S(2)}) copy-start(bf16[512,512]{1,0:T(8,128)(2,1)} %constant.4.clone.second_table) | copy-start | bytes 1572868
  2.1 0.7 copy-start.2
  2.8 0.7 copy-start.3
  3.5 0.7 copy-start.4
  4.1 0.7 copy-start.5
where the time goes:
time: 94.4 us; the launch traced here: 94 us
  Pallas kernels  84.6 us (90%)
  local copies, waits for them, and re-layouts  9.41 us (10%)
    pallas_call x1, Pallas kernels, on_device(): pl.pallas_call(functools.partial(kernel, n), out_shape=jax.ShapeDtypeStru...  84.6 us
    unnamed x13, local copies, waits for them, and re-layouts  9.41 us

commit v1 on v0

--- a/solution.py
+++ b/solution.py
@@ -2,7 +2,6 @@
 
 import jax
 import jax.numpy as jnp
-import numpy as np
 from jax import lax
 from jax.experimental import pallas as pl
 from jax.experimental.pallas import tpu as pltpu
@@ -10,23 +9,23 @@
 
 N3 = 32
 N4 = 16
-CHUNKS = 8
+CHUNKS = 4
 STEP = 16
 PAD = 8
 HALF = 0.5
+RELAY = True
+LIMIT = 28
 
 
 def low_bit(x):
     return x & -x
 
 
-def lift_matrix(count):
-    table = np.eye(count, dtype=np.float64)
-    for j in range(1, count):
-        s = low_bit(j)
-        table[j, j - s] -= 0.5
-        table[j, (j + s) % count] -= 0.5
-    return table
+def lift_entries(j, k, count):
+    s = low_bit(j)
+    zero = jnp.zeros(j.shape, jnp.float32)
+    less = jnp.where(k == j - s, HALF, zero) + jnp.where(k == ((j + s) & (count - 1)), HALF, zero)
+    return jnp.where(j == k, 1.0, zero) - jnp.where(j == 0, zero, less)
 
 
 def three_parts(x):
@@ -44,8 +43,6 @@
     profiles,
     row_gain,
     levels,
-    second_table,
-    merged_table,
     out,
     u,
     diffused,
@@ -59,6 +56,8 @@
     y_right,
     coefs,
     gains,
+    second_table,
+    merged_table,
     local_sem,
     send_sem,
     recv_sem,
@@ -130,9 +129,21 @@
     def relay(c):
         return remote(y_left.at[at(c), :], y_next, c, 3, 2, (me + n - 2) % n)
 
+    def to_coarse(c):
+        return remote(y_right.at[at(c), :], y_left, c, 2 + 2 * n.bit_length(), 3, behind_(n // 4))
+
+    def to_opposite(c):
+        return remote(
+            y_left.at[at(c), :], y_right, c, 3 + 2 * n.bit_length(), 4, (me + n // 2) % n
+        )
+
+    def behind_(by):
+        return (me + n - by) % n
+
     sends = [(even, to_pair), (odd, to_behind)]
+    middle = me == n // 4
     s, slot = 2, 4
-    while s < n:
+    while s < n // 2 if RELAY else s < n:
         sends.append(
             (
                 rank % (2 * s) == 0,
@@ -142,9 +153,12 @@
             )
         )
         if 2 * s < n:
+            holds = rank % (2 * s) == 0
+            if RELAY and 4 * s == n:
+                holds = rank == 0
             sends.append(
                 (
-                    rank % (2 * s) == 0,
+                    holds,
                     functools.partial(
                         own, target=y_right, send=slot + 1, slot=4, device=(me + n - s) % n
                     ),
@@ -163,6 +177,29 @@
 
     each(lambda c: last_plane(c).start())
     each(lambda c: first_plane(c).start())
+
+    def grid(start, size):
+        down = lax.broadcasted_iota(jnp.int32, (16, size), 0) + start
+        return down, lax.broadcasted_iota(jnp.int32, (16, size), 1)
+
+    def second_rows(i, carry):
+        start = pl.multiple_of(i * 16, 16)
+        j, k = grid(start, rows)
+        second_table[pl.ds(start, 16), :] = lift_entries(j, k, rows).astype(jnp.bfloat16)
+        return carry
+
+    bits = N4.bit_length() - 1
+
+    def merged_rows(i, carry):
+        start = pl.multiple_of(i * 16, 16)
+        k, j = grid(start, width)
+        third = lift_entries(j >> bits, k >> bits, N3)
+        fourth = lift_entries(j & (N4 - 1), k & (N4 - 1), N4)
+        merged_table[pl.ds(start, 16), :] = (third * fourth).astype(jnp.bfloat16)
+        return carry
+
+    lax.fori_loop(0, rows // 16, second_rows, 0)
+    lax.fori_loop(0, width // 16, merged_rows, 0)
 
     def power(d):
         return jnp.exp2(jnp.full((1, width), levels[d].astype(jnp.float32), jnp.float32))
@@ -282,7 +319,8 @@
         diffuse(j // (rows // STEP), j % (rows // STEP))
         return carry
 
-    lax.fori_loop(0, planes * (rows // STEP), base, 0, unroll=2)
+    steps = planes * (rows // STEP)
+    lax.fori_loop(0, steps, base, 0, unroll=2)
 
     def inner_plane(q, carry):
         each(lambda c: lift_lanes(q, c))
@@ -299,11 +337,14 @@
     each(first_arrived)
     lift_rows(0)
 
-    for holds, copy in sends:
-
-        @pl.when(holds)
-        def _(copy=copy):
-            each(lambda c: copy(c).start())
+    def send(c):
+        for holds, copy in sends:
+
+            @pl.when(holds)
+            def _(copy=copy):
+                copy(c).start()
+
+    each(send)
 
     def last_arrived(c):
         first_plane(c).wait_recv()
@@ -359,8 +400,16 @@
 
         @pl.when(even & (rank % (n // 2) != 0))
         def _():
-            to_pair(c).wait_recv()
-            own(c, y_right, 2, 4, ahead).wait_recv()
+            if RELAY:
+
+                @pl.when(jnp.logical_not(middle))
+                def _():
+                    to_pair(c).wait_recv()
+                    own(c, y_right, 2, 4, ahead).wait_recv()
+
+            else:
+                to_pair(c).wait_recv()
+                own(c, y_right, 2, 4, ahead).wait_recv()
             result[0, where, :] = lifted[0, where, :] - HALF * (
                 y_left[where, :] + y_right[where, :]
             )
@@ -373,6 +422,15 @@
             to_pair(c).wait_recv()
             relay(c).start()
 
+        if RELAY:
+
+            @pl.when(middle)
+            def _():
+                to_pair(c).wait_recv()
+                to_opposite(c).start()
+                own(c, y_right, 2, 4, ahead).wait_recv()
+                to_coarse(c).start()
+
     pass_on(0)
 
     def turn(c, carry):
@@ -385,7 +443,7 @@
 
     each(lambda c: last_plane(c).wait_send())
     each(lambda c: first_plane(c).wait_send())
-    for holds, copy in [*sends, (odd, relay)]:
+    for holds, copy in [*sends, (odd, relay), *([(middle, to_coarse), (middle, to_opposite)] if RELAY else [])]:
 
         @pl.when(holds)
         def _(copy=copy):
@@ -398,8 +456,6 @@
 def on_device(field, selector, profiles, row_gain, levels):
     planes, rows, width = field.shape
     n = lax.axis_size("split")
-    second_table = jnp.asarray(lift_matrix(rows).astype(jnp.bfloat16))
-    merged_table = jnp.asarray(np.kron(lift_matrix(N3), lift_matrix(N4)).T.astype(jnp.bfloat16))
     kinds = 4 + 2 * n.bit_length()
     plane = pltpu.VMEM((rows, width), jnp.float32)
     block = pltpu.VMEM((planes, rows, width), jnp.float32)
@@ -412,8 +468,6 @@
             pl.BlockSpec(memory_space=pltpu.VMEM),
             pl.BlockSpec(memory_space=pltpu.VMEM),
             pl.BlockSpec(memory_space=pltpu.SMEM),
-            pl.BlockSpec(memory_space=pltpu.VMEM),
-            pl.BlockSpec(memory_space=pltpu.VMEM),
         ],
         out_specs=pl.BlockSpec(memory_space=pl.ANY),
         scratch_shapes=[
@@ -429,13 +483,15 @@
             plane,
             pltpu.VMEM((planes, 8, width), jnp.float32),
             pltpu.VMEM((3, rows, 128), jnp.float32),
+            pltpu.VMEM((rows, rows), jnp.bfloat16),
+            pltpu.VMEM((width, width), jnp.bfloat16),
             pltpu.SemaphoreType.DMA((3,)),
             pltpu.SemaphoreType.DMA((kinds, CHUNKS)),
             pltpu.SemaphoreType.DMA((5, CHUNKS)),
             pltpu.SemaphoreType.DMA((planes, CHUNKS)),
         ],
         compiler_params=pltpu.CompilerParams(
-            collective_id=0, has_side_effects=True, vmem_limit_bytes=50 * 1024 * 1024
+            collective_id=0, has_side_effects=True, vmem_limit_bytes=LIMIT * 1024 * 1024
         ),
         name="step_and_lift",
     )(
@@ -444,8 +500,6 @@
         profiles,
         row_gain.reshape(1, rows),
         levels,
-        second_table,
-        merged_table,
     )
 
 

time: 94.4 us -> 88.8 us (0.941)
  Pallas kernels: 84.6 us -> 81.7 us
  local copies, waits for them, and re-layouts: 9.41 us -> 6.89 us
    pallas_call x1, Pallas kernels: 84.6 us -> 81.7 us  [on_device(): pl.pallas_call(functools.partial(kernel, n), out_shape=jax.ShapeDtypeStru...]
    unnamed x13 -> x11, local copies, waits for them, and re-layouts: 9.41 us -> 6.89 us
where the time goes in v1:
time: 88.8 us; the launch traced here: 88.6 us
  Pallas kernels  81.7 us (92%)
  local copies, waits for them, and re-layouts  6.89 us (8%)
    pallas_call x1, Pallas kernels, on_device(): pl.pallas_call(functools.partial(kernel, n), out_shape=jax.ShapeDtypeStru...  81.7 us
    unnamed x11, local copies, waits for them, and re-layouts  6.89 us

profile of v1, /device:TPU:4, one launch (start us, length us, event | category | flops | bytes accessed | tf_op | source)
XLA Modules:
  0.0 88.6 jit_solution(5309422472881476561)
XLA Ops:
  0.0 0.0 copy-start
  0.0 2.2 %copy-done = f32[4,512,512]{2,1,0:T(8,128)S(1)} copy-done((f32[4,512,512]{2,1,0:T(8,128)S(1)}, f32[4,512,512]{2,1,0:T(8,128)}, u32[]{:S(2)}) %copy-start) | copy-done | bytes 4194328
  2.2 0.0 copy-start.1
  2.2 0.7 copy-done.1
  2.9 0.0 copy-start.2
  2.9 0.7 copy-done.2
  3.6 0.0 copy-start.3
  3.6 0.7 copy-done.3
  4.2 0.0 copy-start.4
  4.2 0.7 copy-done.4
  4.9 81.7 %step_and_lift.1 = f32[4,512,512]{2,1,0:T(8,128)S(1)} custom-call(f32[4,512,512]{2,1,0:T(8,128)S(1)} %copy-done, s32[32]{0:T(128)S(1)} %copy-done.3, f32[4,512]{1,0:T(4,128)S(1)} %copy-done.1, f32[1,512]{1,0:T(1,128)S(1)} %bitcast.1, s32[4]{0:T(128)S(1)} %copy-done.4), custom_call_target="tpu_custom_call" | custom-call | tf_op jit(solution)/shard_map/step_and_lift/pallas_call | solution.py:462
  86.6 2.0 %copy.7 = f32[4,512,512]{2,1,0:T(8,128)} copy(f32[4,512,512]{2,1,0:T(8,128)S(1)} %step_and_lift.1) | data formatting | bytes 8388608
Async XLA Ops:
  0.0 2.2 %copy-start = (f32[4,512,512]{2,1,0:T(8,128)S(1)}, f32[4,512,512]{2,1,0:T(8,128)}, u32[]{:S(2)}) copy-start(f32[4,512,512]{2,1,0:T(8,128)} %field.1) | copy-start | bytes 12582916
  2.2 0.7 copy-start.1
  2.9 0.7 copy-start.2
  3.6 0.7 copy-start.3
  4.2 0.7 copy-start.4
